TPU v7x, 32 devices: a whole 2x2x4 slice. The times are simulated.
32 devices in a mesh: dp: 8 (over z, core), tensor: 4 (over y, x).
Axes of the slice: x: 2, y: 2, z: 4, core: 2. Of those that a mesh axis runs over, the one named last changes fastest.
Arguments:
- tokens: bfloat16 [8, 2048, 2048], P('dp', 'tensor'), may hold values from -6 to 6
- in_weight: bfloat16 [3, 2048, 2048], P(None, 'dp', 'tensor'), may hold values from -0.125 to 0.125
- conv_taps: float32 [3, 2048], replicated, may hold values from -3.5 to 3.5
- out_weight: bfloat16 [2048, 2048], P('tensor', 'dp'), may hold values from -0.125 to 0.125
- gate_weight: bfloat16 [2048, 8192], P('dp', 'tensor'), may hold values from -0.125 to 0.125
- up_weight: bfloat16 [2048, 8192], P('dp', 'tensor'), may hold values from -0.125 to 0.125
- down_weight: bfloat16 [8192, 2048], P('tensor', 'dp'), may hold values from -0.125 to 0.125
- norm_gain1: float32 [2048], replicated, may hold values from 0.1 to 1.9
- norm_gain2: float32 [2048], replicated, may hold values from 0.1 to 1.9
- out_grad: bfloat16 [8, 2048, 2048], P('dp', 'tensor'), may hold values from -6 to 6
Outputs:
- block_out: bfloat16 [8, 2048, 2048], P('dp', 'tensor')
- tokens_grad: float32 [8, 2048, 2048], P('dp', 'tensor')
- in_weight_grad: float32 [3, 2048, 2048], P(None, 'dp', 'tensor')
- conv_taps_grad: float32 [3, 2048], replicated
- out_weight_grad: float32 [2048, 2048], P('tensor', 'dp')
- gate_weight_grad: float32 [2048, 8192], P('dp', 'tensor')
- up_weight_grad: float32 [2048, 8192], P('dp', 'tensor')
- down_weight_grad: float32 [8192, 2048], P('tensor', 'dp')
- gain1_grad: float32 [2048], replicated
- gain2_grad: float32 [2048], replicated
All inputs are finite; a program needn't handle non-finite values.
Results may differ from a plain program's by a relative error of at most 0.015.
Values may be sent and summed in bfloat16 or wider, within the bound.
No kernel may reach another device: no remote copies, remote signals or barrier semaphores. Data moves between devices by JAX's collectives and lax.ppermute only.
A program may use at most 256 MiB of HBM per device.

v0:
```python
import jax
import jax.numpy as jnp
from jax import lax
from jax.sharding import PartitionSpec as P

EPS = 1e-05


def rms_scale(values):
    return lax.rsqrt(jnp.mean(values * values, axis=-1, keepdims=True) + EPS)


def causal_conv(values, taps):
    padded = jnp.pad(values, ((0, 0), (2, 0), (0, 0)))
    return taps[0] * padded[:, :-2] + taps[1] * padded[:, 1:-1] + taps[2] * padded[:, 2:]


def conv_back(grad, values, taps):
    length = grad.shape[1]
    after = jnp.pad(grad, ((0, 0), (0, 2), (0, 0)))
    back = taps[2] * after[:, :-2] + taps[1] * after[:, 1:-1] + taps[0] * after[:, 2:]
    before = jnp.pad(values, ((0, 0), (2, 0), (0, 0)))
    tap_grads = jnp.stack(
        [jnp.sum(grad * before[:, j : j + length], axis=(0, 1)) for j in range(3)]
    )
    return (back, tap_grads)


def norm_back(hidden, scale, gain, grad):
    scaled = gain * grad
    back = scale * scaled - hidden * scale**3 * jnp.mean(scaled * hidden, axis=-1, keepdims=True)
    return (back, jnp.sum(grad * hidden * scale, axis=(0, 1)))


def local(
    tokens,
    in_weight,
    conv_taps,
    out_weight,
    gate_weight,
    up_weight,
    down_weight,
    norm_gain1,
    norm_gain2,
    out_grad,
):
    single_float32 = jnp.float32
    bf16 = jnp.bfloat16
    chans = out_weight.shape[0]
    width = conv_taps.shape[1]
    offset = lax.axis_index("tensor") * chans
    taps = lax.dynamic_slice_in_dim(conv_taps, offset, chans, 1)
    input_weight_complete, output_weight_complete = (
        lax.all_gather(in_weight, "dp", axis=1, tiled=True),
        lax.all_gather(out_weight, "dp", axis=1, tiled=True),
    )
    hidden = tokens.astype(single_float32)
    scale1 = rms_scale(hidden)
    normed = (hidden * scale1 * norm_gain1).astype(bf16)
    first_normed_total = lax.all_gather(normed, "tensor", axis=1, tiled=True)
    projection_rows = jnp.einsum(
        "hpt,vtx->vhpx",
        first_normed_total,
        input_weight_complete,
        preferred_element_type=single_float32,
    )
    bgate, cgate, xgate = (projection_rows[0], projection_rows[1], projection_rows[2])
    mixed_in = bgate * xgate
    conv = causal_conv(mixed_in, taps)
    output_gate = (cgate * conv).astype(bf16)
    branch_partial = jnp.einsum(
        "xbu,um->xbm", output_gate, output_weight_complete, preferred_element_type=single_float32
    )
    branch = lax.psum_scatter(branch_partial, "tensor", scatter_dimension=1, tiled=True)
    second = hidden + branch
    scale2 = rms_scale(second)
    normed2 = (second * scale2 * norm_gain2).astype(bf16)
    second_normed_total = lax.all_gather(normed2, "tensor", axis=1, tiled=True)
    gate_weight_complete, upward_weight_complete, down_weight_complete = (
        lax.all_gather(gate_weight, "dp", axis=0, tiled=True),
        lax.all_gather(up_weight, "dp", axis=0, tiled=True),
        lax.all_gather(down_weight, "dp", axis=1, tiled=True),
    )
    gate_rows = jnp.einsum(
        "gta,am->gtm",
        second_normed_total,
        gate_weight_complete,
        preferred_element_type=single_float32,
    )
    upward_rows = jnp.einsum(
        "gta,am->gtm",
        second_normed_total,
        upward_weight_complete,
        preferred_element_type=single_float32,
    )
    sigma = jax.nn.sigmoid(gate_rows)
    silu_gate = gate_rows * sigma
    activation_rows = (silu_gate * upward_rows).astype(bf16)
    feedforward_partial = jnp.einsum(
        "naw,wx->nax", activation_rows, down_weight_complete, preferred_element_type=single_float32
    )
    ffn = lax.psum_scatter(
        feedforward_partial.astype(jnp.bfloat16), "tensor", scatter_dimension=1, tiled=True
    ).astype(jnp.float32)
    block_out = (second + ffn).astype(bf16)
    (
        input_weight_backward,
        output_weight_backward,
        gate_weight_backward,
        upward_weight_backward,
        down_weight_backward,
    ) = (
        input_weight_complete,
        output_weight_complete,
        gate_weight_complete,
        upward_weight_complete,
        down_weight_complete,
    )
    gradient_total = lax.all_gather(out_grad, "tensor", axis=1, tiled=True)
    down_gradient_rows = jnp.einsum(
        "cxu,cxr->ur", activation_rows, gradient_total, preferred_element_type=single_float32
    )
    activation_gradient = jnp.einsum(
        "bqw,rw->bqr", gradient_total, down_weight_backward, preferred_element_type=single_float32
    )
    gate_gradient = (
        activation_gradient * upward_rows * sigma * (1.0 + gate_rows * (1.0 - sigma))
    ).astype(bf16)
    upper_gradient = (activation_gradient * silu_gate).astype(bf16)
    gate_gradient_rows = jnp.einsum(
        "bkr,bki->ri", second_normed_total, gate_gradient, preferred_element_type=single_float32
    )
    upward_gradient_rows = jnp.einsum(
        "bkr,bki->ri", second_normed_total, upper_gradient, preferred_element_type=single_float32
    )
    second_normed_gradient_partial = jnp.einsum(
        "ovx,ix->ovi", gate_gradient, gate_weight_backward, preferred_element_type=single_float32
    )
    second_normed_gradient_partial = second_normed_gradient_partial + jnp.einsum(
        "ovx,ix->ovi", upper_gradient, upward_weight_backward, preferred_element_type=single_float32
    )
    gate_owned, up_owned, down_owned = (
        lax.psum_scatter(
            gate_gradient_rows.astype(jnp.bfloat16), "dp", scatter_dimension=0, tiled=True
        ).astype(jnp.float32),
        lax.psum_scatter(
            upward_gradient_rows.astype(jnp.bfloat16), "dp", scatter_dimension=0, tiled=True
        ).astype(jnp.float32),
        lax.psum_scatter(
            down_gradient_rows.astype(jnp.bfloat16), "dp", scatter_dimension=1, tiled=True
        ).astype(jnp.float32),
    )
    dnormed2 = lax.psum_scatter(
        second_normed_gradient_partial, "tensor", scatter_dimension=1, tiled=True
    )
    dsecond_norm, gain2_part = norm_back(second, scale2, norm_gain2, dnormed2)
    dsecond = out_grad.astype(single_float32) + dsecond_norm
    branch_gradient_total = lax.all_gather(dsecond.astype(bf16), "tensor", axis=1, tiled=True)
    output_weight_gradient = jnp.einsum(
        "jez,jeb->zb", output_gate, branch_gradient_total, preferred_element_type=single_float32
    )
    output_gate_gradient = jnp.einsum(
        "abk,fk->abf",
        branch_gradient_total,
        output_weight_backward,
        preferred_element_type=single_float32,
    )
    dcgate = output_gate_gradient * conv
    dconv = output_gate_gradient * cgate
    dmixed, tap_part = conv_back(dconv, mixed_in, taps)
    projection_gradient = jnp.stack([dmixed * xgate, dcgate, dmixed * bgate]).astype(bf16)
    input_weight_gradient = jnp.einsum(
        "htz,mhtg->mzg",
        first_normed_total,
        projection_gradient,
        preferred_element_type=single_float32,
    )
    first_normed_gradient_partial = jnp.einsum(
        "ohrs,ons->hrn",
        projection_gradient,
        input_weight_backward,
        preferred_element_type=single_float32,
    )
    in_owned, out_owned = (
        lax.psum_scatter(
            input_weight_gradient.astype(jnp.bfloat16), "dp", scatter_dimension=1, tiled=True
        ).astype(jnp.float32),
        lax.psum_scatter(
            output_weight_gradient.astype(jnp.bfloat16), "dp", scatter_dimension=1, tiled=True
        ).astype(jnp.float32),
    )
    dnormed = lax.psum_scatter(
        first_normed_gradient_partial.astype(jnp.bfloat16),
        "tensor",
        scatter_dimension=1,
        tiled=True,
    ).astype(jnp.float32)
    dhidden_norm, gain1_part = norm_back(hidden, scale1, norm_gain1, dnormed)
    tokens_grad = dsecond + dhidden_norm
    tap_wide = lax.dynamic_update_slice_in_dim(
        jnp.zeros((3, width), single_float32), tap_part, offset, 1
    )
    tap_total, gain1_total, gain2_total = lax.psum(
        (tap_wide, gain1_part, gain2_part), ("dp", "tensor")
    )
    return (
        block_out,
        tokens_grad,
        in_owned,
        tap_total,
        out_owned,
        gate_owned,
        up_owned,
        down_owned,
        gain1_total,
        gain2_total,
    )


def solution(mesh):
    in_specs = (
        P("dp", "tensor", None),
        P(None, "dp", "tensor"),
        P(),
        P("tensor", "dp"),
        P("dp", "tensor"),
        P("dp", "tensor"),
        P("tensor", "dp"),
        P(),
        P(),
        P("dp", "tensor", None),
    )
    out_specs = (
        P("dp", "tensor", None),
        P("dp", "tensor", None),
        P(None, "dp", "tensor"),
        P(),
        P("tensor", "dp"),
        P("dp", "tensor"),
        P("dp", "tensor"),
        P("tensor", "dp"),
        P(),
        P(),
    )
    return jax.shard_map(local, mesh=mesh, in_specs=in_specs, out_specs=out_specs, check_vma=False)
```

profile of v0, /device:TPU:0, one launch (start us, length us, event | category | flops | bytes accessed | tf_op | source)
XLA Modules:
  0.0 1739.9 jit_solution(10525292303862076047)
XLA Ops:
  7.2 0.7 all-gather.12.cloned.1.call-update
  8.0 2.1 fusion.36
  10.0 0.6 multiply_multiply_fusion
  10.6 0.6 copy-done.12
  11.2 2.6 fusion.38
  13.8 0.7 all-gather.14.cloned.1.call-update
  14.6 0.9 constant_dynamic-slice_fusion
  15.5 61.6 %all-gather.12.cloned.1.call-done = bf16[3,2048,512]{2,1,0:T(8,128)(2,1)} async-done(((bf16[3,256,512]{2,1,0:T(8,128)(2,1)}), bf16[3,2048,512]{2,1,0:T(8,128)(2,1)}) %all-gather.12.cloned.1.call-update) | async-done | bytes 6291472 | tf_op jit(solution)/shard_map/all_gather | solution.py:54
  77.1 88.7 %all-gather.10.cloned.1.call-done = bf16[1,2048,2048]{2,1,0:T(8,128)(2,1)} async-done(((bf16[1,512,2048]{2,1,0:T(8,128)(2,1)}), bf16[1,2048,2048]{2,1,0:T(8,128)(2,1)}) %all-gather.10.cloned.1.call-update) | async-done | bytes 8388624 | tf_op jit(solution)/shard_map/all_gather | solution.py:60
  165.8 17.4 fusion.19
  183.2 1.1 bitcast_multiply_fusion.5
  184.3 3.3 copy-done
  187.7 1.5 copy-done.5
  189.1 3.6 fusion.52
  192.7 5.6 all-gather.14.cloned.1.call-done
  198.3 12.5 convolution_bitcast_fusion
  211.6 152.2 %reduce-scatter.10.cloned.1.call-done = f32[1,512,2048]{2,1,0:T(8,128)} async-done(((f32[1,2048,2048]{2,1,0:T(8,128)}), f32[1,512,2048]{2,1,0:T(8,128)}) %reduce-scatter.10.cloned.1.call-update) | async-done | bytes 4194320 | tf_op jit(solution)/shard_map/reduce_scatter | solution.py:74
  363.9 2.8 multiply_reduce_fusion.4
  366.7 0.6 multiply_multiply_fusion.1
  367.3 1.3 copy-done.1
  368.6 1.7 multiply_convert_fusion.3
  370.5 0.7 all-gather.18.cloned.1.call-update
  371.2 0.7 all-gather.24.cloned.1.call-update
  372.0 0.7 all-gather.22.cloned.1.call-update
  372.7 74.7 %all-gather.20.cloned.1.call-done = bf16[2048,2048]{1,0:T(8,128)(2,1)} async-done(((bf16[256,2048]{1,0:T(8,128)(2,1)}), bf16[2048,2048]{1,0:T(8,128)(2,1)}) %all-gather.20.cloned.1.call-update) | async-done | bytes 8388624 | tf_op jit(solution)/shard_map/all_gather | solution.py:81
  447.4 88.4 %all-gather.16.cloned.1.call-done = bf16[1,2048,2048]{2,1,0:T(8,128)(2,1)} async-done(((bf16[1,512,2048]{2,1,0:T(8,128)(2,1)}), bf16[1,2048,2048]{2,1,0:T(8,128)(2,1)}) %all-gather.16.cloned.1.call-update) | async-done | bytes 8388624 | tf_op jit(solution)/shard_map/all_gather | solution.py:78
  535.9 24.2 %fusion.13 = f32[2048,2048]{1,0:T(8,128)} fusion(bf16[2048,2048]{1,0:T(8,128)(2,1)} %all-gather.20.cloned.1.call-done, bf16[1,2048,2048]{2,1,0:T(8,128)(2,1)} %all-gather.16.cloned.1.call-done), kind=kOutput, calls=%fused_computation.26 | convolution fusion | flops 17179869184 | bytes 33554432 | tf_op jit(solution)/shard_map/gta,am->gtm/dot_general | solution.py:90
  560.0 59.5 %all-gather.18.cloned.1.call-done = bf16[2048,2048]{1,0:T(8,128)(2,1)} async-done(((bf16[256,2048]{1,0:T(8,128)(2,1)}), bf16[2048,2048]{1,0:T(8,128)(2,1)}) %all-gather.18.cloned.1.call-update) | async-done | bytes 8388624 | tf_op jit(solution)/shard_map/all_gather | solution.py:80
  619.5 24.2 %fusion.15 = f32[2048,2048]{1,0:T(8,128)} fusion(bf16[2048,2048]{1,0:T(8,128)(2,1)} %all-gather.18.cloned.1.call-done, bf16[1,2048,2048]{2,1,0:T(8,128)(2,1)} %all-gather.16.cloned.1.call-done), kind=kOutput, calls=%fused_computation.28 | convolution fusion | flops 17179869184 | bytes 33554432 | tf_op jit(solution)/shard_map/gta,am->gtm/dot_general | solution.py:84
  643.7 63.9 %all-gather.24.cloned.1.call-done = bf16[1,2048,2048]{2,1,0:T(8,128)(2,1)} async-done(((bf16[1,512,2048]{2,1,0:T(8,128)(2,1)}), bf16[1,2048,2048]{2,1,0:T(8,128)(2,1)}) %all-gather.24.cloned.1.call-update) | async-done | bytes 8388624 | tf_op jit(solution)/shard_map/all_gather | solution.py:119
  707.6 84.1 %all-gather.22.cloned.1.call-done = bf16[2048,2048]{1,0:T(8,128)(2,1)} async-done(((bf16[2048,256]{1,0:T(8,128)(2,1)}), bf16[2048,2048]{1,0:T(8,128)(2,1)}) %all-gather.22.cloned.1.call-update) | async-done | bytes 8388624 | tf_op jit(solution)/shard_map/all_gather | solution.py:82
  791.7 36.7 %multiply_convert_fusion = (bf16[2048,2048]{1,0:T(8,128)(2,1)}, bf16[2048,2048]{1,0:T(8,128)(2,1)}, bf16[2048,2048]{1,0:T(8,128)(2,1)}) fusion(f32[2048,2048]{1,0:T(8,128)} %fusion.15, f32[2048,2048]{1,0:T(8,128)} %fusion.13, bf16[2048,2048]{1,0:T(8,128)(2,1)} %all-gather.22.cloned.1.call-done, bf16[1,2048,2048]{2,1,0:T(8,128)(2,1)} %all-gather.24.cloned.1.call-done), kind=kOutput, calls=%fused_computation.2 | convolution fusion | flops 17242783744 | bytes 75497472 | tf_op jit(solution)/shard_map/bqw,rw->bqr/dot_general | solution.py:123
  828.3 24.3 %fusion.57 = f32[2048,2048]{1,0:T(8,128)} fusion(bf16[2048,2048]{1,0:T(8,128)(2,1)} %get-tuple-element.39, bf16[2048,2048]{1,0:T(8,128)(2,1)} %all-gather.18.cloned.1.call-done), kind=kOutput, calls=%fused_computation.91 | convolution fusion | flops 17179869184 | bytes 33554432 | tf_op jit(solution)/shard_map/ovx,ix->ovi/dot_general | solution.py:136
  852.6 26.7 %add_bitcast_fusion = f32[1,2048,2048]{2,1,0:T(8,128)} fusion(f32[2048,2048]{1,0:T(8,128)} %fusion.57, bf16[2048,2048]{1,0:T(8,128)(2,1)} %get-tuple-element.38, bf16[2048,2048]{1,0:T(8,128)(2,1)} %all-gather.20.cloned.1.call-done), kind=kOutput, calls=%fused_computation.1 | convolution fusion | flops 17184063488 | bytes 50331648 | tf_op jit(solution)/shard_map/ovx,ix->ovi/dot_general | solution.py:139
  879.4 23.7 %convert_bitcast_fusion = bf16[1,2048,2048]{2,1,0:T(8,128)(2,1)} fusion(bf16[2048,2048]{1,0:T(8,128)(2,1)} %get-tuple-element.40, bf16[2048,2048]{1,0:T(8,128)(2,1)} %all-gather.22.cloned.1.call-done), kind=kOutput, calls=%fused_computation.34 | convolution fusion | flops 17184063488 | bytes 25165824 | tf_op jit(solution)/shard_map/naw,wx->nax/dot_general | solution.py:99
  903.2 128.4 %reduce-scatter.14.cloned.1.call-done = f32[1,512,2048]{2,1,0:T(8,128)} async-done(((f32[1,2048,2048]{2,1,0:T(8,128)}), f32[1,512,2048]{2,1,0:T(8,128)}) %reduce-scatter.14.cloned.1.call-update) | async-done | bytes 4194320 | tf_op jit(solution)/shard_map/reduce_scatter | solution.py:153
  1031.6 5.1 multiply_reduce_fusion
  1036.7 84.4 %reduce-scatter.12.cloned.1.call-done = bf16[1,512,2048]{2,1,0:T(8,128)(2,1)} async-done(((bf16[1,2048,2048]{2,1,0:T(8,128)(2,1)}), bf16[1,512,2048]{2,1,0:T(8,128)(2,1)}) %reduce-scatter.12.cloned.1.call-update) | async-done | bytes 2097168 | tf_op jit(solution)/shard_map/reduce_scatter | solution.py:102
  1121.1 6.8 fusion.56
  1127.9 23.9 %fusion.21 = bf16[2048,2048]{1,0:T(8,128)(2,1)} fusion(bf16[2048,2048]{1,0:T(8,128)(2,1)} %get-tuple-element.39, bf16[1,2048,2048]{2,1,0:T(8,128)(2,1)} %all-gather.16.cloned.1.call-done), kind=kOutput, calls=%fused_computation.35 | convolution fusion | flops 17184063488 | bytes 25165824 | tf_op jit(solution)/shard_map/bkr,bki->ri/dot_general | solution.py:130
  1151.9 23.8 %fusion.24 = bf16[2048,2048]{1,0:T(8,128)(2,1)} fusion(bf16[2048,2048]{1,0:T(8,128)(2,1)} %get-tuple-element.38, bf16[1,2048,2048]{2,1,0:T(8,128)(2,1)} %all-gather.16.cloned.1.call-done), kind=kOutput, calls=%fused_computation.36 | convolution fusion | flops 17184063488 | bytes 25165824 | tf_op jit(solution)/shard_map/bkr,bki->ri/dot_general | solution.py:133
  1175.7 24.0 %fusion.27 = bf16[2048,2048]{1,0:T(8,128)(2,1)} fusion(bf16[2048,2048]{1,0:T(8,128)(2,1)} %get-tuple-element.40, bf16[1,2048,2048]{2,1,0:T(8,128)(2,1)} %all-gather.24.cloned.1.call-done), kind=kOutput, calls=%fused_computation.37 | convolution fusion | flops 17184063488 | bytes 25165824 | tf_op jit(solution)/shard_map/cxu,cxr->ur/dot_general | solution.py:120
  1199.8 15.8 all-gather.26.cloned.1.call-done
  1215.6 9.1 fusion.49
  1224.9 15.0 multiply_reduce_fusion.2
  1239.9 5.2 fusion.46
  1245.1 3.7 fusion.47
  1248.8 17.6 %convert_bitcast_fusion.1 = bf16[3,2048,512]{1,2,0:T(8,128)(2,1)} fusion(bf16[1,2048,2048]{2,1,0:T(8,128)(2,1)} %all-gather.10.cloned.1.call-done, bf16[1,2048,512]{2,1,0:T(8,128)(2,1)S(1)} %fusion.47, bf16[1,2048,512]{2,1,0:T(8,128)(2,1)S(1)} %get-tuple-element.41, bf16[1,2048,512]{2,1,0:T(8,128)(2,1)S(1)} %get-tuple-element.30), kind=kOutput, calls=%fused_computation.40 | convolution fusion | flops 12894339072 | bytes 20971520 | tf_op jit(solution)/shard_map/htz,mhtg->mzg/dot_general | solution.py:172
  1266.5 18.8 %fusion.30 = bf16[1,2048,2048]{2,1,0:T(8,128)(2,1)} fusion(bf16[3,2048,512]{2,1,0:T(8,128)(2,1)} %all-gather.12.cloned.1.call-done, bf16[1,2048,512]{2,1,0:T(8,128)(2,1)S(1)} %fusion.47, bf16[1,2048,512]{2,1,0:T(8,128)(2,1)} %copy-done.25, bf16[1,2048,512]{2,1,0:T(8,128)(2,1)} %copy-done.8), kind=kOutput, calls=%fused_computation.38 | convolution fusion | flops 12895387648 | bytes 20971520 | tf_op jit(solution)/shard_map/ohrs,ons->hrn/dot_general | solution.py:178
  1285.4 22.3 %reduce-scatter.22.cloned.1.call-done = bf16[256,2048]{1,0:T(8,128)(2,1)} async-done(((bf16[2048,2048]{1,0:T(8,128)(2,1)}), bf16[256,2048]{1,0:T(8,128)(2,1)}) %reduce-scatter.22.cloned.1.call-update) | async-done | bytes 1048592 | tf_op jit(solution)/shard_map/reduce_scatter | solution.py:143
  1307.7 2.8 convert_element_type.116
  1310.5 87.4 %reduce-scatter.24.cloned.1.call-done = bf16[256,2048]{1,0:T(8,128)(2,1)} async-done(((bf16[2048,2048]{1,0:T(8,128)(2,1)}), bf16[256,2048]{1,0:T(8,128)(2,1)}) %reduce-scatter.24.cloned.1.call-update) | async-done | bytes 1048592 | tf_op jit(solution)/shard_map/reduce_scatter | solution.py:146
  1397.9 2.8 convert_element_type.118
  1400.7 87.4 %reduce-scatter.26.cloned.1.call-done = bf16[2048,256]{1,0:T(8,128)(2,1)} async-done(((bf16[2048,2048]{1,0:T(8,128)(2,1)}), bf16[2048,256]{1,0:T(8,128)(2,1)}) %reduce-scatter.26.cloned.1.call-update) | async-done | bytes 1048592 | tf_op jit(solution)/shard_map/reduce_scatter | solution.py:149
  1488.1 2.7 convert_element_type.120
  1490.8 5.7 fusion.43
  1496.6 28.0 %reduce-scatter.20.cloned.1.call-done = bf16[512,256]{1,0:T(8,128)(2,1)} async-done(((bf16[512,2048]{1,0:T(8,128)(2,1)}), bf16[512,256]{1,0:T(8,128)(2,1)}) %reduce-scatter.20.cloned.1.call-update) | async-done | bytes 262160 | tf_op jit(solution)/shard_map/reduce_scatter | solution.py:188
  1524.6 1.8 convert_element_type.114
  1526.4 68.9 %reduce-scatter.18.cloned.1.call-done = bf16[3,256,512]{1,2,0:T(8,128)(2,1)} async-done(((bf16[3,2048,512]{1,2,0:T(8,128)(2,1)}), bf16[3,256,512]{1,2,0:T(8,128)(2,1)}) %reduce-scatter.18.cloned.1.call-update) | async-done | bytes 786448 | tf_op jit(solution)/shard_map/reduce_scatter | solution.py:185
  1595.3 2.6 copy.24
  1597.9 85.5 %reduce-scatter.16.cloned.1.call-done = bf16[1,512,2048]{2,1,0:T(8,128)(2,1)} async-done(((bf16[1,2048,2048]{2,1,0:T(8,128)(2,1)}), bf16[1,512,2048]{2,1,0:T(8,128)(2,1)}) %reduce-scatter.16.cloned.1.call-update) | async-done | bytes 2097168 | tf_op jit(solution)/shard_map/reduce_scatter | solution.py:192
  1683.3 3.2 fusion.42
  1686.5 40.3 %all-reduce.2 = (f32[3,2048]{1,0:T(4,128)}, f32[2048]{0:T(1024)}, f32[2048]{0:T(1024)}) all-reduce(f32[3,2048]{1,0:T(4,128)S(1)} %maximum_dynamic-update-slice_fusion, f32[2048]{0:T(1024)S(1)} %get-tuple-element.24, f32[2048]{0:T(1024)S(1)} %copy-done.14), channel_id=1, replica_groups=mesh['dp'=8,'tensor'=4] {'dp','tensor'}, use_global_device_ids=true, to_apply=%region_12.13 | all-reduce | flops 10240 | bytes 81920 | tf_op jit(solution)/shard_map/psum | solution.py:203
  1726.8 6.0 fusion.35
  (83 shorter events, 1.8 us)
Async XLA Ops:
  7.2 4.0 copy-start.2
  7.2 69.9 %all-gather.12.cloned.1.call-start = ((), (), s32[]{:S(2)}) async-start(), calls=%async_computation.10 | async-start | bytes 7077888 | tf_op jit(solution)/shard_map/all_gather | solution.py:54
  7.9 157.9 %all-gather.10.cloned.1.call-start = ((), (), s32[]{:S(2)}) async-start(), calls=%async_computation.9 | async-start | bytes 10485760 | tf_op jit(solution)/shard_map/all_gather | solution.py:60
  10.6 0.6 copy-start.12
  13.8 184.5 %all-gather.14.cloned.1.call-start = ((), (), s32[]{:S(2)}) async-start(), calls=%async_computation.11 | async-start | bytes 2359296 | tf_op jit(solution)/shard_map/all_gather | solution.py:55
  14.5 349.3 %reduce-scatter.10.cloned.1.call-start = ((), (), s32[]{:S(2)}) async-start(), calls=%async_computation.12 | async-start | bytes 20971520 | tf_op jit(solution)/shard_map/reduce_scatter | solution.py:74
  15.5 168.8 %copy-start.17 = (f32[1,512]{1,0:T(1,128)}, f32[1,512]{1,0:T(1,128)S(1)}, u32[]{:S(2)}) copy-start(f32[1,512]{1,0:T(1,128)S(1)} %get-tuple-element.43) | copy-start | bytes 6148
  15.5 168.8 %copy-start.19 = (f32[1,512]{1,0:T(1,128)}, f32[1,512]{1,0:T(1,128)S(1)}, u32[]{:S(2)}) copy-start(f32[1,512]{1,0:T(1,128)S(1)} %get-tuple-element.44) | copy-start | bytes 6148
  15.5 168.8 %copy-start.21 = (f32[1,512]{1,0:T(1,128)}, f32[1,512]{1,0:T(1,128)S(1)}, u32[]{:S(2)}) copy-start(f32[1,512]{1,0:T(1,128)S(1)} %get-tuple-element.45) | copy-start | bytes 6148
  183.2 4.5 copy-start
  184.3 4.8 copy-start.5
  210.8 236.6 %all-gather.20.cloned.1.call-start = ((), (), s32[]{:S(2)}) async-start(), calls=%async_computation.15 | async-start | bytes 9437184 | tf_op jit(solution)/shard_map/all_gather | solution.py:81
  211.4 157.2 %copy-start.9 = (f32[2048]{0:T(1024)S(1)}, f32[2048]{0:T(1024)}, u32[]{:S(2)}) copy-start(f32[2048]{0:T(1024)} %param.18) | copy-start | bytes 24580
  211.4 324.4 %all-gather.16.cloned.1.call-start = ((), (), s32[]{:S(2)}) async-start(), calls=%async_computation.13 | async-start | bytes 10485760 | tf_op jit(solution)/shard_map/all_gather | solution.py:78
  366.7 2.0 copy-start.1
  367.3 1.3 copy-start.15
  370.4 249.1 %all-gather.18.cloned.1.call-start = ((), (), s32[]{:S(2)}) async-start(), calls=%async_computation.14 | async-start | bytes 9437184 | tf_op jit(solution)/shard_map/all_gather | solution.py:80
  371.2 336.4 %all-gather.24.cloned.1.call-start = ((), (), s32[]{:S(2)}) async-start(), calls=%async_computation.18 | async-start | bytes 10485760 | tf_op jit(solution)/shard_map/all_gather | solution.py:119
  371.9 419.8 %all-gather.22.cloned.1.call-start = ((), (), s32[]{:S(2)}) async-start(), calls=%async_computation.16 | async-start | bytes 9437184 | tf_op jit(solution)/shard_map/all_gather | solution.py:82
  372.6 658.9 %reduce-scatter.14.cloned.1.call-start = ((), (), s32[]{:S(2)}) async-start(), calls=%async_computation.19 | async-start | bytes 20971520 | tf_op jit(solution)/shard_map/reduce_scatter | solution.py:153
  879.4 241.7 %reduce-scatter.12.cloned.1.call-start = ((), (), s32[]{:S(2)}) async-start(), calls=%async_computation.17 | async-start | bytes 10485760 | tf_op jit(solution)/shard_map/reduce_scatter | solution.py:102
  903.1 128.5 %copy-start.10 = (f32[2048]{0:T(1024)S(1)}, f32[2048]{0:T(1024)}, u32[]{:S(2)}) copy-start(f32[2048]{0:T(1024)} %param.18) | copy-start | bytes 24580
  903.1 128.5 %copy-start.16 = (f32[512]{0:T(512)S(1)}, f32[512]{0:T(512)}, u32[]{:S(2)}) copy-start(f32[512]{0:T(512)} %copy-done.15) | copy-start | bytes 6148
  903.1 218.0 %copy-start.6 = (bf16[1,512,2048]{2,1,0:T(8,128)(2,1)S(1)}, bf16[1,512,2048]{2,1,0:T(8,128)(2,1)}, u32[]{:S(2)}) copy-start(bf16[1,512,2048]{2,1,0:T(8,128)(2,1)} %param.19) | copy-start | bytes 6291460
  903.1 218.0 %copy-start.23 = (f32[512]{0:T(512)S(1)}, f32[512]{0:T(512)}, u32[]{:S(2)}) copy-start(f32[512]{0:T(512)} %get-tuple-element.48) | copy-start | bytes 6148
  903.1 312.5 %all-gather.26.cloned.1.call-start = ((), (), s32[]{:S(2)}) async-start(), calls=%async_computation.20 | async-start | bytes 10485760 | tf_op jit(solution)/shard_map/all_gather | solution.py:158
  1127.9 179.8 %reduce-scatter.22.cloned.1.call-start = ((), (), s32[]{:S(2)}) async-start(), calls=%async_computation.24 | async-start | bytes 9437184 | tf_op jit(solution)/shard_map/reduce_scatter | solution.py:143
  1151.8 246.1 %reduce-scatter.24.cloned.1.call-start = ((), (), s32[]{:S(2)}) async-start(), calls=%async_computation.25 | async-start | bytes 9437184 | tf_op jit(solution)/shard_map/reduce_scatter | solution.py:146
  1175.7 312.5 %reduce-scatter.26.cloned.1.call-start = ((), (), s32[]{:S(2)}) async-start(), calls=%async_computation.26 | async-start | bytes 9437184 | tf_op jit(solution)/shard_map/reduce_scatter | solution.py:149
  1199.7 15.9 copy-start.7
  1199.7 324.8 %reduce-scatter.20.cloned.1.call-start = ((), (), s32[]{:S(2)}) async-start(), calls=%async_computation.23 | async-start | bytes 2359296 | tf_op jit(solution)/shard_map/reduce_scatter | solution.py:188
  1224.8 370.5 %reduce-scatter.18.cloned.1.call-start = ((), (), s32[]{:S(2)}) async-start(), calls=%async_computation.22 | async-start | bytes 7077888 | tf_op jit(solution)/shard_map/reduce_scatter | solution.py:185
  1224.8 15.0 copy-start.18
  1224.8 15.0 copy-start.20
  1224.9 15.0 copy-start.22
  1239.8 5.3 copy-start.4
  1239.8 9.0 copy-start.25
  1245.1 3.7 copy-start.8
  1266.5 416.8 %reduce-scatter.16.cloned.1.call-start = ((), (), s32[]{:S(2)}) async-start(), calls=%async_computation.21 | async-start | bytes 10485760 | tf_op jit(solution)/shard_map/reduce_scatter | solution.py:192
  1490.8 192.5 %copy-start.11 = (f32[2048]{0:T(1024)S(1)}, f32[2048]{0:T(1024)}, u32[]{:S(2)}) copy-start(f32[2048]{0:T(1024)} %param.17) | copy-start | bytes 24580
  1490.8 192.5 %copy-start.13 = (f32[512]{0:T(512)S(1)}, f32[512]{0:T(512)}, u32[]{:S(2)}) copy-start(f32[512]{0:T(512)} %copy-done.12) | copy-start | bytes 6148
  1496.5 186.8 %copy-start.3 = (bf16[1,512,2048]{2,1,0:T(8,128)(2,1)S(1)}, bf16[1,512,2048]{2,1,0:T(8,128)(2,1)}, u32[]{:S(2)}) copy-start(bf16[1,512,2048]{2,1,0:T(8,128)(2,1)} %param.10) | copy-start | bytes 6291460
  1496.6 190.0 %copy-start.14 = (f32[2048]{0:T(1024)S(1)}, f32[2048]{0:T(1024)}, u32[]{:S(2)}) copy-start(f32[2048]{0:T(1024)} %get-tuple-element.20) | copy-start | bytes 24580
  1496.6 230.3 %copy-start.24 = (f32[512]{0:T(512)S(1)}, f32[512]{0:T(512)}, u32[]{:S(2)}) copy-start(f32[512]{0:T(512)} %get-tuple-element.46) | copy-start | bytes 6148
Sparse Core Ops, SparseCore 0:
  9.6 67.4 all-gather.11
  79.5 86.2 all-gather.9
  167.4 30.8 all-gather.13
  210.9 152.8 reduce-scatter.9
  365.3 82.0 all-gather.19
  449.7 86.1 all-gather.15
  537.4 82.0 all-gather.17
  621.4 86.1 all-gather.23
  709.2 82.4 all-gather.21
  879.5 152.0 reduce-scatter.13
  1034.6 86.4 reduce-scatter.11
  1128.0 87.5 all-gather.25
  1218.0 89.6 reduce-scatter.21
  1309.9 87.9 reduce-scatter.23
  1400.2 87.9 reduce-scatter.25
  1490.4 34.1 reduce-scatter.19
  1526.9 68.4 reduce-scatter.17
  1598.5 84.7 reduce-scatter.15
where the time goes:
time: 1750 us; the launch traced here: 1740 us
  waiting for transfers between devices  1290 us (74%)
  matrix products  322 us (18%)
  other arithmetic  60.8 us (3%)
  blocking collectives  40.3 us (2%)
    reduce_scatter x1, waiting for transfers between devices, local(): lax.psum_scatter(branch_partial, 'tensor', scatter_dimension=1, tiled=True)  152 us
    reduce_scatter x1, waiting for transfers between devices, local(): lax.psum_scatter(second_normed_gradient_partial, 'tensor', scatter_dimens...  128 us
    all_gather x1, waiting for transfers between devices, local(): first_normed_total = lax.all_gather(normed, 'tensor', axis=1, tiled=True)  88.7 us
    all_gather x1, waiting for transfers between devices, local(): second_normed_total = lax.all_gather(normed2, 'tensor', axis=1, tiled=True)  88.4 us
    reduce_scatter x1, waiting for transfers between devices, local(): lax.psum_scatter(upward_gradient_rows.astype(jnp.bfloat16), 'dp', scatter...  87.4 us
    reduce_scatter x1, waiting for transfers between devices, local(): lax.psum_scatter(down_gradient_rows.astype(jnp.bfloat16), 'dp', scatter_d...  87.4 us
    reduce_scatter x1, waiting for transfers between devices, local(): lax.psum_scatter(first_normed_gradient_partial.astype(jnp.bfloat16), 'ten...  85.5 us
    reduce_scatter x1, waiting for transfers between devices, local(): lax.psum_scatter(feedforward_partial.astype(jnp.bfloat16), 'tensor', scat...  84.4 us
  transfers between devices with their start and end apart: 18, of which 18 were waited for; matrix products, arithmetic and copies ran while one was open for 16% of the time, Pallas kernels for 0%

commit v1 on v0

--- a/solution.py
+++ b/solution.py
@@ -4,6 +4,18 @@
 from jax.sharding import PartitionSpec as P
 
 EPS = 1e-05
+
+
+def gather_by_bits(x, axis, dim):
+    ways, here = (lax.axis_size(axis), lax.axis_index(axis))
+    grown, reach = (x, 1)
+    while reach < ways:
+        theirs = lax.ppermute(grown, axis, [(d, d ^ reach) for d in range(ways)])
+        mine_first = jnp.concatenate([grown, theirs], axis=dim)
+        theirs_first = jnp.concatenate([theirs, grown], axis=dim)
+        grown = jnp.where(here & reach == 0, mine_first, theirs_first)
+        reach = 2 * reach
+    return grown
 
 
 def rms_scale(values):
@@ -78,7 +90,7 @@
     second_normed_total = lax.all_gather(normed2, "tensor", axis=1, tiled=True)
     gate_weight_complete, upward_weight_complete, down_weight_complete = (
         lax.all_gather(gate_weight, "dp", axis=0, tiled=True),
-        lax.all_gather(up_weight, "dp", axis=0, tiled=True),
+        gather_by_bits(up_weight, "dp", 0),
         lax.all_gather(down_weight, "dp", axis=1, tiled=True),
     )
     gate_rows = jnp.einsum(

time: 1750 us -> 1820 us (1.040)
  waiting for transfers between devices: 1290 us -> 1340 us
    all_gather x1, waiting for transfers between devices: 84.1 us -> 173 us  [local(): lax.all_gather(down_weight, 'dp', axis=1, tiled=True)]
    all_gather x1 -> x0, waiting for transfers between devices: 74.7 us -> none  [local(): lax.all_gather(up_weight, 'dp', axis=0, tiled=True)]
    ppermute x0 -> x3, waiting for transfers between devices: none -> 49 us  [gather_by_bits(): theirs = lax.ppermute(grown, axis, [(d, d ^ reach) for d in range(ways)])]
    all_gather x1, waiting for transfers between devices: 63.9 us -> 21.5 us  [local(): gradient_total = lax.all_gather(out_grad, 'tensor', axis=1, tiled=True)]
    all_gather x1, waiting for transfers between devices: 59.5 us -> 92.1 us  [local(): lax.all_gather(gate_weight, 'dp', axis=0, tiled=True)]
  transfers between devices with their start and end apart: 18 -> 20, of which waited for: 18 -> 19; matrix products, arithmetic and copies ran while one was open for 16% -> 15% of each run, Pallas kernels for 0% -> 0%
where the time goes in v1:
time: 1820 us; the launch traced here: 1810 us
  waiting for transfers between devices  1340 us (74%)
  matrix products  323 us (18%)
  other arithmetic  68.8 us (4%)
  blocking collectives  40.3 us (2%)
    all_gather x1, waiting for transfers between devices, local(): lax.all_gather(down_weight, 'dp', axis=1, tiled=True)  173 us
    reduce_scatter x1, waiting for transfers between devices, local(): lax.psum_scatter(branch_partial, 'tensor', scatter_dimension=1, tiled=True)  151 us
    reduce_scatter x1, waiting for transfers between devices, local(): lax.psum_scatter(second_normed_gradient_partial, 'tensor', scatter_dimens...  130 us
    all_gather x1, waiting for transfers between devices, local(): lax.all_gather(gate_weight, 'dp', axis=0, tiled=True)  92.1 us
    all_gather x1, waiting for transfers between devices, local(): first_normed_total = lax.all_gather(normed, 'tensor', axis=1, tiled=True)  88.7 us
    all_gather x1, waiting for transfers between devices, local(): second_normed_total = lax.all_gather(normed2, 'tensor', axis=1, tiled=True)  88.5 us
    reduce_scatter x1, waiting for transfers between devices, local(): lax.psum_scatter(upward_gradient_rows.astype(jnp.bfloat16), 'dp', scatter...  87.6 us
    reduce_scatter x1, waiting for transfers between devices, local(): lax.psum_scatter(down_gradient_rows.astype(jnp.bfloat16), 'dp', scatter_d...  87.5 us
  transfers between devices with their start and end apart: 20, of which 19 were waited for; matrix products, arithmetic and copies ran while one was open for 15% of the time, Pallas kernels for 0%

profile of v1, /device:TPU:0, one launch (start us, length us, event | category | flops | bytes accessed | tf_op | source)
XLA Modules:
  0.0 1806.6 jit_solution(9540009023758743625)
XLA Ops:
  7.2 0.7 all-gather.11.cloned.1.call-update
  8.0 2.1 fusion.36
  11.2 2.6 fusion.38
  13.8 0.7 all-gather.13.cloned.1.call-update
  14.6 0.9 constant_dynamic-slice_fusion
  15.5 61.6 %all-gather.11.cloned.1.call-done = bf16[3,2048,512]{2,1,0:T(8,128)(2,1)} async-done(((bf16[3,256,512]{2,1,0:T(8,128)(2,1)}), bf16[3,2048,512]{2,1,0:T(8,128)(2,1)}) %all-gather.11.cloned.1.call-update) | async-done | bytes 6291472 | tf_op jit(solution)/shard_map/all_gather | solution.py:66
  77.1 88.7 %all-gather.9.cloned.1.call-done = bf16[1,2048,2048]{2,1,0:T(8,128)(2,1)} async-done(((bf16[1,512,2048]{2,1,0:T(8,128)(2,1)}), bf16[1,2048,2048]{2,1,0:T(8,128)(2,1)}) %all-gather.9.cloned.1.call-update) | async-done | bytes 8388624 | tf_op jit(solution)/shard_map/all_gather | solution.py:72
  165.8 17.4 fusion.19
  183.2 1.1 bitcast_multiply_fusion.5
  184.3 3.3 copy-done
  187.7 1.5 copy-done.5
  189.1 3.6 fusion.52
  192.7 5.6 all-gather.13.cloned.1.call-done
  198.3 12.5 convolution_bitcast_fusion
  212.0 0.7 all-gather.17.cloned.1.call-update
  213.0 150.9 %reduce-scatter.10.cloned.1.call-done = f32[1,512,2048]{2,1,0:T(8,128)} async-done(((f32[1,2048,2048]{2,1,0:T(8,128)}), f32[1,512,2048]{2,1,0:T(8,128)}) %reduce-scatter.10.cloned.1.call-update) | async-done | bytes 4194320 | tf_op jit(solution)/shard_map/reduce_scatter | solution.py:86
  363.9 2.8 multiply_reduce_fusion.4
  367.3 1.3 copy-done.1
  368.7 1.7 multiply_convert_fusion.3
  370.6 2.8 collective-permute-done
  373.3 2.7 maximum_select_fusion.2
  376.1 1.6 collective-permute-start.1
  377.7 46.3 %collective-permute-done.1 = bf16[512,2048]{1,0:T(8,128)(2,1)} collective-permute-done((bf16[512,2048]{1,0:T(8,128)(2,1)S(1)}, bf16[512,2048]{1,0:T(8,128)(2,1)}, u32[]{:S(2)}, u32[]{:S(2)}) %collective-permute-start.1) | collective-permute-done | bytes 2097184 | tf_op jit(solution)/shard_map/ppermute | solution.py:13
  423.9 5.3 maximum_select_fusion.1
  429.2 2.5 collective-permute-start.2
  431.7 21.5 %all-gather.21.cloned.1.call-done = bf16[1,2048,2048]{2,1,0:T(8,128)(2,1)} async-done(((bf16[1,512,2048]{2,1,0:T(8,128)(2,1)}), bf16[1,2048,2048]{2,1,0:T(8,128)(2,1)}) %all-gather.21.cloned.1.call-update) | async-done | bytes 8388624 | tf_op jit(solution)/shard_map/all_gather | solution.py:131
  453.2 173.4 %all-gather.19.cloned.1.call-done = bf16[2048,2048]{1,0:T(8,128)(2,1)} async-done(((bf16[2048,256]{1,0:T(8,128)(2,1)}), bf16[2048,2048]{1,0:T(8,128)(2,1)}) %all-gather.19.cloned.1.call-update) | async-done | bytes 8388624 | tf_op jit(solution)/shard_map/all_gather | solution.py:94
  626.6 24.4 %fusion.7 = f32[2048,2048]{1,0:T(8,128)} fusion(bf16[2048,2048]{1,0:T(8,128)(2,1)} %all-gather.19.cloned.1.call-done, bf16[1,2048,2048]{2,1,0:T(8,128)(2,1)} %all-gather.21.cloned.1.call-done), kind=kOutput, calls=%fused_computation.21 | convolution fusion | flops 17179869184 | bytes 33554432 | tf_op jit(solution)/shard_map/bqw,rw->bqr/dot_general | solution.py:135
  651.0 92.1 %all-gather.17.cloned.1.call-done = bf16[2048,2048]{1,0:T(8,128)(2,1)} async-done(((bf16[256,2048]{1,0:T(8,128)(2,1)}), bf16[2048,2048]{1,0:T(8,128)(2,1)}) %all-gather.17.cloned.1.call-update) | async-done | bytes 8388624 | tf_op jit(solution)/shard_map/all_gather | solution.py:92
  743.1 88.5 %all-gather.15.cloned.1.call-done = bf16[1,2048,2048]{2,1,0:T(8,128)(2,1)} async-done(((bf16[1,512,2048]{2,1,0:T(8,128)(2,1)}), bf16[1,2048,2048]{2,1,0:T(8,128)(2,1)}) %all-gather.15.cloned.1.call-update) | async-done | bytes 8388624 | tf_op jit(solution)/shard_map/all_gather | solution.py:90
  831.5 24.2 %fusion.15 = f32[2048,2048]{1,0:T(8,128)} fusion(bf16[2048,2048]{1,0:T(8,128)(2,1)} %all-gather.17.cloned.1.call-done, bf16[1,2048,2048]{2,1,0:T(8,128)(2,1)} %all-gather.15.cloned.1.call-done), kind=kOutput, calls=%fused_computation.29 | convolution fusion | flops 17179869184 | bytes 33554432 | tf_op jit(solution)/shard_map/gta,am->gtm/dot_general | solution.py:96
  855.8 36.6 %multiply_convert_fusion = (bf16[2048,2048]{1,0:T(8,128)(2,1)}, bf16[2048,2048]{1,0:T(8,128)(2,1)}, bf16[2048,2048]{1,0:T(8,128)(2,1)}) fusion(f32[2048,2048]{1,0:T(8,128)} %fusion.7, f32[2048,2048]{1,0:T(8,128)} %fusion.15, bf16[1024,2048]{1,0:T(8,128)(2,1)} %collective-permute-done.2, bf16[1024,2048]{1,0:T(8,128)(2,1)} %maximum_select_fusion.1, ...), kind=kOutput, calls=%fused_computation.2 | convolution fusion | flops 17280532480 | bytes 75497472 | tf_op jit(solution)/shard_map/gta,am->gtm/dot_general | solution.py:102
  892.4 24.4 %fusion.59 = f32[2048,2048]{1,0:T(8,128)} fusion(bf16[2048,2048]{1,0:T(8,128)(2,1)} %get-tuple-element.39, bf16[2048,2048]{1,0:T(8,128)(2,1)} %all-gather.17.cloned.1.call-done), kind=kOutput, calls=%fused_computation.96 | convolution fusion | flops 17179869184 | bytes 33554432 | tf_op jit(solution)/shard_map/ovx,ix->ovi/dot_general | solution.py:148
  916.8 27.7 %add_bitcast_fusion = f32[1,2048,2048]{2,1,0:T(8,128)} fusion(f32[2048,2048]{1,0:T(8,128)} %fusion.59, bf16[2048,2048]{1,0:T(8,128)(2,1)} %get-tuple-element.38, bf16[1024,2048]{1,0:T(8,128)(2,1)} %collective-permute-done.2, bf16[1024,2048]{1,0:T(8,128)(2,1)} %maximum_select_fusion.1, pred[]{:T(512)S(6)} %eq.9), kind=kOutput, calls=%fused_computation.1 | convolution fusion | flops 17221812224 | bytes 50331648 | tf_op jit(solution)/shard_map/ovx,ix->ovi/dot_general | solution.py:151
  944.6 23.6 %convert_bitcast_fusion = bf16[1,2048,2048]{2,1,0:T(8,128)(2,1)} fusion(bf16[2048,2048]{1,0:T(8,128)(2,1)} %get-tuple-element.40, bf16[2048,2048]{1,0:T(8,128)(2,1)} %all-gather.19.cloned.1.call-done), kind=kOutput, calls=%fused_computation.35 | convolution fusion | flops 17184063488 | bytes 25165824 | tf_op jit(solution)/shard_map/naw,wx->nax/dot_general | solution.py:111
  968.4 130.2 %reduce-scatter.14.cloned.1.call-done = f32[1,512,2048]{2,1,0:T(8,128)} async-done(((f32[1,2048,2048]{2,1,0:T(8,128)}), f32[1,512,2048]{2,1,0:T(8,128)}) %reduce-scatter.14.cloned.1.call-update) | async-done | bytes 4194320 | tf_op jit(solution)/shard_map/reduce_scatter | solution.py:165
  1098.6 5.1 multiply_reduce_fusion
  1103.7 84.2 %reduce-scatter.12.cloned.1.call-done = bf16[1,512,2048]{2,1,0:T(8,128)(2,1)} async-done(((bf16[1,2048,2048]{2,1,0:T(8,128)(2,1)}), bf16[1,512,2048]{2,1,0:T(8,128)(2,1)}) %reduce-scatter.12.cloned.1.call-update) | async-done | bytes 2097168 | tf_op jit(solution)/shard_map/reduce_scatter | solution.py:114
  1187.9 6.8 fusion.58
  1194.8 23.9 %fusion.21 = bf16[2048,2048]{1,0:T(8,128)(2,1)} fusion(bf16[2048,2048]{1,0:T(8,128)(2,1)} %get-tuple-element.39, bf16[1,2048,2048]{2,1,0:T(8,128)(2,1)} %all-gather.15.cloned.1.call-done), kind=kOutput, calls=%fused_computation.36 | convolution fusion | flops 17184063488 | bytes 25165824 | tf_op jit(solution)/shard_map/bkr,bki->ri/dot_general | solution.py:142
  1218.8 23.8 %fusion.24 = bf16[2048,2048]{1,0:T(8,128)(2,1)} fusion(bf16[2048,2048]{1,0:T(8,128)(2,1)} %get-tuple-element.38, bf16[1,2048,2048]{2,1,0:T(8,128)(2,1)} %all-gather.15.cloned.1.call-done), kind=kOutput, calls=%fused_computation.37 | convolution fusion | flops 17184063488 | bytes 25165824 | tf_op jit(solution)/shard_map/bkr,bki->ri/dot_general | solution.py:145
  1242.6 24.0 %fusion.27 = bf16[2048,2048]{1,0:T(8,128)(2,1)} fusion(bf16[2048,2048]{1,0:T(8,128)(2,1)} %get-tuple-element.40, bf16[1,2048,2048]{2,1,0:T(8,128)(2,1)} %all-gather.21.cloned.1.call-done), kind=kOutput, calls=%fused_computation.38 | convolution fusion | flops 17184063488 | bytes 25165824 | tf_op jit(solution)/shard_map/cxu,cxr->ur/dot_general | solution.py:132
  1266.7 15.8 all-gather.23.cloned.1.call-done
  1282.5 9.1 fusion.49
  1291.7 14.9 multiply_reduce_fusion.2
  1306.7 5.2 fusion.46
  1311.9 3.7 fusion.47
  1315.6 17.6 convert_bitcast_fusion.1
  1333.3 18.8 %fusion.30 = bf16[1,2048,2048]{2,1,0:T(8,128)(2,1)} fusion(bf16[3,2048,512]{2,1,0:T(8,128)(2,1)} %all-gather.11.cloned.1.call-done, bf16[1,2048,512]{2,1,0:T(8,128)(2,1)S(1)} %fusion.47, bf16[1,2048,512]{2,1,0:T(8,128)(2,1)} %copy-done.26, bf16[1,2048,512]{2,1,0:T(8,128)(2,1)} %copy-done.8), kind=kOutput, calls=%fused_computation.39 | convolution fusion | flops 12895387648 | bytes 20971520 | tf_op jit(solution)/shard_map/ohrs,ons->hrn/dot_general | solution.py:190
  1352.2 22.2 %reduce-scatter.22.cloned.1.call-done = bf16[256,2048]{1,0:T(8,128)(2,1)} async-done(((bf16[2048,2048]{1,0:T(8,128)(2,1)}), bf16[256,2048]{1,0:T(8,128)(2,1)}) %reduce-scatter.22.cloned.1.call-update) | async-done | bytes 1048592 | tf_op jit(solution)/shard_map/reduce_scatter | solution.py:155
  1374.3 2.8 convert_element_type.116
  1377.1 87.6 %reduce-scatter.24.cloned.1.call-done = bf16[256,2048]{1,0:T(8,128)(2,1)} async-done(((bf16[2048,2048]{1,0:T(8,128)(2,1)}), bf16[256,2048]{1,0:T(8,128)(2,1)}) %reduce-scatter.24.cloned.1.call-update) | async-done | bytes 1048592 | tf_op jit(solution)/shard_map/reduce_scatter | solution.py:158
  1464.8 2.8 convert_element_type.118
  1467.5 87.5 %reduce-scatter.26.cloned.1.call-done = bf16[2048,256]{1,0:T(8,128)(2,1)} async-done(((bf16[2048,2048]{1,0:T(8,128)(2,1)}), bf16[2048,256]{1,0:T(8,128)(2,1)}) %reduce-scatter.26.cloned.1.call-update) | async-done | bytes 1048592 | tf_op jit(solution)/shard_map/reduce_scatter | solution.py:161
  1555.0 2.7 convert_element_type.120
  1557.7 5.7 fusion.43
  1563.5 28.0 %reduce-scatter.20.cloned.1.call-done = bf16[512,256]{1,0:T(8,128)(2,1)} async-done(((bf16[512,2048]{1,0:T(8,128)(2,1)}), bf16[512,256]{1,0:T(8,128)(2,1)}) %reduce-scatter.20.cloned.1.call-update) | async-done | bytes 262160 | tf_op jit(solution)/shard_map/reduce_scatter | solution.py:200
  1591.5 1.8 convert_element_type.114
  1593.2 69.1 %reduce-scatter.18.cloned.1.call-done = bf16[3,256,512]{1,2,0:T(8,128)(2,1)} async-done(((bf16[3,2048,512]{1,2,0:T(8,128)(2,1)}), bf16[3,256,512]{1,2,0:T(8,128)(2,1)}) %reduce-scatter.18.cloned.1.call-update) | async-done | bytes 786448 | tf_op jit(solution)/shard_map/reduce_scatter | solution.py:197
  1662.3 2.6 copy.24
  1664.8 85.5 %reduce-scatter.16.cloned.1.call-done = bf16[1,512,2048]{2,1,0:T(8,128)(2,1)} async-done(((bf16[1,2048,2048]{2,1,0:T(8,128)(2,1)}), bf16[1,512,2048]{2,1,0:T(8,128)(2,1)}) %reduce-scatter.16.cloned.1.call-update) | async-done | bytes 2097168 | tf_op jit(solution)/shard_map/reduce_scatter | solution.py:204
  1750.3 3.2 fusion.42
  1753.5 40.3 %all-reduce.2 = (f32[3,2048]{1,0:T(4,128)}, f32[2048]{0:T(1024)}, f32[2048]{0:T(1024)}) all-reduce(f32[3,2048]{1,0:T(4,128)S(1)} %maximum_dynamic-update-slice_fusion, f32[2048]{0:T(1024)S(1)} %get-tuple-element.24, f32[2048]{0:T(1024)S(1)} %copy-done.15), channel_id=1, replica_groups=mesh['dp'=8,'tensor'=4] {'dp','tensor'}, use_global_device_ids=true, to_apply=%region_12.13 | all-reduce | flops 10240 | bytes 81920 | tf_op jit(solution)/shard_map/psum | solution.py:215
  1793.8 6.0 fusion.35
  (90 shorter events, 4.1 us)
Async XLA Ops:
  7.2 4.0 copy-start.2
  7.2 69.9 %all-gather.11.cloned.1.call-start = ((), (), s32[]{:S(2)}) async-start(), calls=%async_computation.10 | async-start | bytes 7077888 | tf_op jit(solution)/shard_map/all_gather | solution.py:66
  7.9 157.9 %all-gather.9.cloned.1.call-start = ((), (), s32[]{:S(2)}) async-start(), calls=%async_computation.9 | async-start | bytes 10485760 | tf_op jit(solution)/shard_map/all_gather | solution.py:72
  10.6 0.6 copy-start.13
  13.8 184.5 %all-gather.13.cloned.1.call-start = ((), (), s32[]{:S(2)}) async-start(), calls=%async_computation.11 | async-start | bytes 2359296 | tf_op jit(solution)/shard_map/all_gather | solution.py:67
  14.5 349.3 %reduce-scatter.10.cloned.1.call-start = ((), (), s32[]{:S(2)}) async-start(), calls=%async_computation.12 | async-start | bytes 20971520 | tf_op jit(solution)/shard_map/reduce_scatter | solution.py:86
  15.5 168.8 %copy-start.18 = (f32[1,512]{1,0:T(1,128)}, f32[1,512]{1,0:T(1,128)S(1)}, u32[]{:S(2)}) copy-start(f32[1,512]{1,0:T(1,128)S(1)} %get-tuple-element.43) | copy-start | bytes 6148
  15.5 168.8 %copy-start.20 = (f32[1,512]{1,0:T(1,128)}, f32[1,512]{1,0:T(1,128)S(1)}, u32[]{:S(2)}) copy-start(f32[1,512]{1,0:T(1,128)S(1)} %get-tuple-element.44) | copy-start | bytes 6148
  15.5 168.8 %copy-start.22 = (f32[1,512]{1,0:T(1,128)}, f32[1,512]{1,0:T(1,128)S(1)}, u32[]{:S(2)}) copy-start(f32[1,512]{1,0:T(1,128)S(1)} %get-tuple-element.45) | copy-start | bytes 6148
  183.2 4.5 copy-start
  184.3 4.9 copy-start.5
  210.8 242.4 %all-gather.21.cloned.1.call-start = ((), (), s32[]{:S(2)}) async-start(), calls=%async_computation.17 | async-start | bytes 10485760 | tf_op jit(solution)/shard_map/all_gather | solution.py:131
  211.4 415.1 %all-gather.19.cloned.1.call-start = ((), (), s32[]{:S(2)}) async-start(), calls=%async_computation.15 | async-start | bytes 9437184 | tf_op jit(solution)/shard_map/all_gather | solution.py:94
  212.0 531.1 %all-gather.17.cloned.1.call-start = ((), (), s32[]{:S(2)}) async-start(), calls=%async_computation.14 | async-start | bytes 9437184 | tf_op jit(solution)/shard_map/all_gather | solution.py:92
  212.7 155.9 %copy-start.10 = (f32[2048]{0:T(1024)S(1)}, f32[2048]{0:T(1024)}, u32[]{:S(2)}) copy-start(f32[2048]{0:T(1024)} %param.18) | copy-start | bytes 24580
  212.8 618.8 %all-gather.15.cloned.1.call-start = ((), (), s32[]{:S(2)}) async-start(), calls=%async_computation.13 | async-start | bytes 10485760 | tf_op jit(solution)/shard_map/all_gather | solution.py:90
  366.7 2.0 copy-start.1
  367.3 1.3 copy-start.16
  368.7 1.8 copy-start.9
  370.4 728.1 %reduce-scatter.14.cloned.1.call-start = ((), (), s32[]{:S(2)}) async-start(), calls=%async_computation.18 | async-start | bytes 20971520 | tf_op jit(solution)/shard_map/reduce_scatter | solution.py:165
  370.5 2.9 collective-permute-start
  376.1 47.9 %collective-permute-start.1 = (bf16[512,2048]{1,0:T(8,128)(2,1)S(1)}, bf16[512,2048]{1,0:T(8,128)(2,1)}, u32[]{:S(2)}, u32[]{:S(2)}) collective-permute-start(bf16[512,2048]{1,0:T(8,128)(2,1)S(1)} %maximum_select_fusion.2), channel_id=1, source_target_pairs={{0,8},{4,12},{8,0},{12,4},{16,24},{20,28},{24,16},{28,20},{1,9},{5... | collective-permute-start | bytes 6291464 | tf_op jit(solution)/shard_map/ppermute | solution.py:13
  429.2 426.5 %collective-permute-start.2 = (bf16[1024,2048]{1,0:T(8,128)(2,1)}, bf16[1024,2048]{1,0:T(8,128)(2,1)}, u32[]{:S(2)}, u32[]{:S(2)}) collective-permute-start(bf16[1024,2048]{1,0:T(8,128)(2,1)} %maximum_select_fusion.1), channel_id=1, source_target_pairs={{0,16},{4,20},{8,24},{12,28},{16,0},{20,4},{24,8},{28,12},{1,17},{... | collective-permute-start | bytes 12582920 | tf_op jit(solution)/shard_map/ppermute | solution.py:13
  944.6 243.3 %reduce-scatter.12.cloned.1.call-start = ((), (), s32[]{:S(2)}) async-start(), calls=%async_computation.16 | async-start | bytes 10485760 | tf_op jit(solution)/shard_map/reduce_scatter | solution.py:114
  968.3 130.3 %copy-start.11 = (f32[2048]{0:T(1024)S(1)}, f32[2048]{0:T(1024)}, u32[]{:S(2)}) copy-start(f32[2048]{0:T(1024)} %param.18) | copy-start | bytes 24580
  968.3 130.3 %copy-start.17 = (f32[512]{0:T(512)S(1)}, f32[512]{0:T(512)}, u32[]{:S(2)}) copy-start(f32[512]{0:T(512)} %copy-done.16) | copy-start | bytes 6148
  968.3 219.6 %copy-start.6 = (bf16[1,512,2048]{2,1,0:T(8,128)(2,1)S(1)}, bf16[1,512,2048]{2,1,0:T(8,128)(2,1)}, u32[]{:S(2)}) copy-start(bf16[1,512,2048]{2,1,0:T(8,128)(2,1)} %param.19) | copy-start | bytes 6291460
  968.3 219.6 %copy-start.24 = (f32[512]{0:T(512)S(1)}, f32[512]{0:T(512)}, u32[]{:S(2)}) copy-start(f32[512]{0:T(512)} %get-tuple-element.48) | copy-start | bytes 6148
  968.3 314.1 %all-gather.23.cloned.1.call-start = ((), (), s32[]{:S(2)}) async-start(), calls=%async_computation.19 | async-start | bytes 10485760 | tf_op jit(solution)/shard_map/all_gather | solution.py:170
  1194.7 179.6 %reduce-scatter.22.cloned.1.call-start = ((), (), s32[]{:S(2)}) async-start(), calls=%async_computation.23 | async-start | bytes 9437184 | tf_op jit(solution)/shard_map/reduce_scatter | solution.py:155
  1218.7 246.0 %reduce-scatter.24.cloned.1.call-start = ((), (), s32[]{:S(2)}) async-start(), calls=%async_computation.24 | async-start | bytes 9437184 | tf_op jit(solution)/shard_map/reduce_scatter | solution.py:158
  1242.6 312.4 %reduce-scatter.26.cloned.1.call-start = ((), (), s32[]{:S(2)}) async-start(), calls=%async_computation.25 | async-start | bytes 9437184 | tf_op jit(solution)/shard_map/reduce_scatter | solution.py:161
  1266.6 15.8 copy-start.7
  1266.7 324.8 %reduce-scatter.20.cloned.1.call-start = ((), (), s32[]{:S(2)}) async-start(), calls=%async_computation.22 | async-start | bytes 2359296 | tf_op jit(solution)/shard_map/reduce_scatter | solution.py:200
  1291.6 370.7 %reduce-scatter.18.cloned.1.call-start = ((), (), s32[]{:S(2)}) async-start(), calls=%async_computation.21 | async-start | bytes 7077888 | tf_op jit(solution)/shard_map/reduce_scatter | solution.py:197
  1291.6 15.0 copy-start.19
  1291.7 15.0 copy-start.21
  1291.7 15.0 copy-start.23
  1306.6 5.3 copy-start.4
  1306.6 9.0 copy-start.26
  1311.9 3.7 copy-start.8
  1333.3 417.0 %reduce-scatter.16.cloned.1.call-start = ((), (), s32[]{:S(2)}) async-start(), calls=%async_computation.20 | async-start | bytes 10485760 | tf_op jit(solution)/shard_map/reduce_scatter | solution.py:204
  1557.7 192.6 %copy-start.12 = (f32[2048]{0:T(1024)S(1)}, f32[2048]{0:T(1024)}, u32[]{:S(2)}) copy-start(f32[2048]{0:T(1024)} %param.17) | copy-start | bytes 24580
  1557.7 192.6 %copy-start.14 = (f32[512]{0:T(512)S(1)}, f32[512]{0:T(512)}, u32[]{:S(2)}) copy-start(f32[512]{0:T(512)} %copy-done.13) | copy-start | bytes 6148
  1563.4 186.9 %copy-start.3 = (bf16[1,512,2048]{2,1,0:T(8,128)(2,1)S(1)}, bf16[1,512,2048]{2,1,0:T(8,128)(2,1)}, u32[]{:S(2)}) copy-start(bf16[1,512,2048]{2,1,0:T(8,128)(2,1)} %param.10) | copy-start | bytes 6291460
  1563.4 190.1 %copy-start.15 = (f32[2048]{0:T(1024)S(1)}, f32[2048]{0:T(1024)}, u32[]{:S(2)}) copy-start(f32[2048]{0:T(1024)} %get-tuple-element.20) | copy-start | bytes 24580
  1563.4 230.4 %copy-start.25 = (f32[512]{0:T(512)S(1)}, f32[512]{0:T(512)}, u32[]{:S(2)}) copy-start(f32[512]{0:T(512)} %get-tuple-element.46) | copy-start | bytes 6148
Sparse Core Ops, SparseCore 0:
  9.6 67.4 all-gather.10
  79.5 86.2 all-gather.8
  167.4 30.8 all-gather.12
  210.9 152.8 reduce-scatter.9
  365.6 87.6 all-gather.20
  454.7 171.8 all-gather.18
  628.2 114.8 all-gather.16
  745.5 86.0 all-gather.14
  944.7 153.8 reduce-scatter.13
  1101.5 86.3 reduce-scatter.11
  1194.8 87.5 all-gather.22
  1284.7 89.5 reduce-scatter.21
  1376.7 87.9 reduce-scatter.23
  1467.0 87.9 reduce-scatter.25
  1557.3 34.1 reduce-scatter.19
  1593.7 68.5 reduce-scatter.17
  1665.5 84.7 reduce-scatter.15
